TPU v7x, 256 devices: a whole 4x4x8 slice. The times are simulated.
256 devices in a mesh: leaf: 64 (over x, z, core), blk: 4 (over y).
Axes of the slice: x: 4, y: 4, z: 8, core: 2. Of those that a mesh axis runs over, the one named last changes fastest.
Arguments:
- features: float32 [64, 262144], P(None, ('leaf', 'blk')), may hold values from -6 to 6
- sketch: float32 [256, 262144], P(None, ('leaf', 'blk')), may hold values from -12 to 12
- omega: float32 [256, 262144], P(None, ('leaf', 'blk')), may hold values from -6 to 6
- slot: int32 [262144], P(('leaf', 'blk')), may hold values from 0 to 262143, as said below
- column_order: int32 [6, 256], replicated, may hold values from 0 to 255, each once within a row
Outputs:
- leaf_basis: float32 [256, 262144], P(None, ('leaf', 'blk'))
- transfers: float32 [64, 6, 512, 256], P('leaf')
Inputs may be any that keep to these rules, and one draw needn't show every extreme that they name: slot is a permutation of all points; a point goes to a device with the same blk index as its own, and every device sends exactly 1024 // 64 of its points to each leaf index.
All inputs are finite; a program needn't handle non-finite values.
Results may differ from a plain program's by a relative error of at most 0.0003.
Values sent between devices are 32-bit elements; how exact they have to be, the bound alone decides.
A program may use at most 128 MiB of HBM per device.

v0:
```python
import math

import jax
import jax.numpy as jnp
from jax import lax
from jax.sharding import PartitionSpec as P


def partner(block, axis, stride):
    count = lax.axis_size(axis)
    route = []
    for low in range(count):
        high = low | 1 << stride
        if high != low and high < count:
            route += [(low, high), (high, low)]
    return lax.ppermute(block, axis, route)


def kernel_block(row_feat, col_feat):
    width = row_feat.shape[0]
    inner = lax.dot_general(
        row_feat,
        col_feat,
        (((0,), (0,)), ((), ())),
        precision=lax.Precision.HIGHEST,
        preferred_element_type=jnp.float32,
    )
    norms_a = jnp.sum(row_feat * row_feat, axis=0)
    norms_b = jnp.sum(col_feat * col_feat, axis=0)
    distance = norms_a[:, None] + norms_b[None, :] - 2.0 * inner
    return jnp.exp(distance * (-2.0 / width))


def per_device(features, sketch, omega, slot, column_order):
    points = features.shape[1]
    rank = sketch.shape[0]
    blk_count = lax.axis_size("blk")
    leaf_count = lax.axis_size("leaf")
    sending = jnp.argsort(slot)
    sorted_slot = slot[sending]
    position_row = (sorted_slot % points).astype(jnp.float32)[None, :]
    received = (
        lax.all_to_all(features[:, sending], "leaf", split_axis=1, concat_axis=1, tiled=True),
        lax.all_to_all(sketch[:, sending], "leaf", split_axis=1, concat_axis=1, tiled=True),
        lax.all_to_all(omega[:, sending], "leaf", split_axis=1, concat_axis=1, tiled=True),
        lax.all_to_all(position_row, "leaf", split_axis=1, concat_axis=1, tiled=True),
    )
    arrived_pos = received[3][0].astype(jnp.int32)
    inverse = jnp.argsort(arrived_pos)
    tree_feat = received[0][:, inverse]
    tree_sketch = received[1][:, inverse]
    tree_omega = received[2][:, inverse]
    kernel = kernel_block(lax.all_gather(tree_feat, "blk", axis=1, tiled=True), tree_feat)
    near_field = jnp.dot(
        lax.all_gather(tree_omega, "blk", axis=1, tiled=True),
        kernel,
        precision=lax.Precision.HIGHEST,
        preferred_element_type=jnp.float32,
    )
    off_sketch = tree_sketch - near_field
    local_gram = lax.dot_general(
        off_sketch,
        off_sketch,
        (((1,), (1,)), ((), ())),
        precision=lax.Precision.HIGHEST,
        preferred_element_type=jnp.float32,
    )
    gram = lax.psum(local_gram, "blk")
    lower = jnp.linalg.cholesky(gram)
    basis_t = lax.linalg.triangular_solve(lower, off_sketch, left_side=True, lower=True)
    leaf_basis = basis_t * math.sqrt(points * blk_count)
    factor = jnp.transpose(lower)
    leaf_id = lax.axis_index("leaf")
    depth = leaf_count.bit_length() - 1
    collected = []
    for height in range(depth):
        sibling = partner(factor, "leaf", height)
        is_second = leaf_id >> height & 1 == 1
        upper_half = jnp.where(is_second, sibling, factor)
        lower_half = jnp.where(is_second, factor, sibling)
        stacked = jnp.concatenate([upper_half, lower_half], axis=0)
        stacked = jnp.take(stacked, column_order[height], axis=1)
        merge_gram = lax.dot_general(
            stacked,
            stacked,
            (((0,), (0,)), ((), ())),
            precision=lax.Precision.HIGHEST,
            preferred_element_type=jnp.float32,
        )
        merge_lower = jnp.linalg.cholesky(merge_gram)
        ortho_t = lax.linalg.triangular_solve(
            merge_lower, jnp.transpose(stacked), left_side=True, lower=True
        )
        collected.append(jnp.transpose(ortho_t) * math.sqrt(2 * rank))
        factor = jnp.transpose(merge_lower)
    transfers = jnp.stack(collected, axis=0)[None]
    return (leaf_basis, transfers)


def solution(mesh):
    placed = (
        P(None, ("leaf", "blk")),
        P(None, ("leaf", "blk")),
        P(None, ("leaf", "blk")),
        P(("leaf", "blk")),
        P(),
    )
    return jax.shard_map(
        per_device,
        mesh=mesh,
        in_specs=placed,
        out_specs=(P(None, ("leaf", "blk")), P("leaf", None, None, None)),
        check_vma=False,
    )
```

profile of v0, /device:TPU:6, one launch (start us, length us, event | category | flops | bytes accessed | tf_op | source)
XLA Modules:
  0.0 720.6 jit_solution(5015356655026021489)
XLA Ops:
  8.1 5.1 sort.31
  13.2 5.7 gather_fusion.1
  19.8 12.2 %all-to-all-start.1 = ((f32[1,64,16]{2,0,1:T(1,128)}), f32[1,64,16]{2,0,1:T(1,128)S(1)}, u32[]{:S(2)}, u32[]{:S(2)}) async-start(f32[1,64,16]{2,0,1:T(1,128)} %copy.69), calls=%async_computation.1 | async-start | bytes 65536 | tf_op jit(solution)/shard_map/all_to_all | solution.py:46
  32.2 2.8 gather_fusion.5
  36.0 3.4 all-to-all-done.1
  39.5 6.9 all-to-all-start.3
  46.7 4.7 gather_fusion.3
  51.4 6.5 all-to-all-done.3
  57.9 6.5 all-to-all-start.2
  64.6 4.4 sort.32
  70.9 4.0 gather_fusion.6
  75.0 16.1 %all-to-all-done.2 = f32[256,64,16]{0,2,1:T(8,128)S(1)} async-done(((f32[256,64,16]{0,2,1:T(8,128)}), f32[256,64,16]{0,2,1:T(8,128)S(1)}, u32[]{:S(2)}, u32[]{:S(2)}) %all-to-all-start.2) | async-done | bytes 1048608 | tf_op jit(solution)/shard_map/all_to_all | solution.py:45
  91.0 4.7 gather_fusion.4
  96.1 4.7 gather_fusion
  100.8 8.1 %all-to-all-start = ((f32[256,64,16]{0,2,1:T(8,128)}), f32[256,64,16]{0,2,1:T(8,128)S(1)}, u32[]{:S(2)}, u32[]{:S(2)}) async-start(f32[256,64,16]{0,2,1:T(8,128)} %bitcast.1), calls=%async_computation | async-start | bytes 2097152 | tf_op jit(solution)/shard_map/all_to_all | solution.py:44
  109.5 26.0 %all-to-all-done = f32[256,64,16]{0,2,1:T(8,128)S(1)} async-done(((f32[256,64,16]{0,2,1:T(8,128)}), f32[256,64,16]{0,2,1:T(8,128)S(1)}, u32[]{:S(2)}, u32[]{:S(2)}) %all-to-all-start) | async-done | bytes 1048608 | tf_op jit(solution)/shard_map/all_to_all | solution.py:44
  135.5 3.5 gather_fusion.2
  140.3 2.4 multiply_reduce_fusion
  142.7 16.0 %fusion.119 = f32[4096,1024]{1,0:T(8,128)} fusion(f32[64,4096]{0,1:T(8,128)S(1)} %copy-done, f32[1024,64]{1,0:T(8,128)S(1)} %copy-done.1), kind=kOutput, calls=%fused_computation.296 | convolution fusion | flops 3221225472 | bytes 18087936 | tf_op jit(solution)/shard_map/dot_general | solution.py:21
  158.7 4.1 all-gather.5.cloned.1.call-done
  162.9 34.6 %fusion.10 = f32[256,1024]{1,0:T(8,128)S(1)} fusion(f32[256,4096]{0,1:T(8,128)} %all-gather.5.cloned.1.call-done, f32[4096,1024]{1,0:T(8,128)} %fusion.119, f32[1024]{0:T(1024)S(1)} %multiply_reduce_fusion.1, f32[4096]{0:T(1024)S(1)} %multiply_reduce_fusion, f32[1024,256]{0,1:T(8,128)S(1)} %copy-done.4), kind=kOutput, calls=%fused_computation.38 | convolution fusion | flops 12901941248 | bytes 23089152 | tf_op jit(solution)/shard_map/dot_general | solution.py:54
  197.5 1.7 fusion.120
  199.3 47.3 %all-reduce.3.cloned.1.call-done = f32[256,256]{0,1:T(8,128)} async-done(((f32[256,256]{0,1:T(8,128)}), f32[256,256]{0,1:T(8,128)}) %all-reduce.3.cloned.1.call-update) | async-done | bytes 262160 | tf_op jit(solution)/shard_map/psum | solution.py:68
  248.6 11.7 %cholesky.340 = f32[128,128]{1,0:T(8,128)S(1)} custom-call(f32[128,128]{1,0:T(8,128)S(1)} %cholesky.574), custom_call_target="Cholesky" | custom-call | tf_op jit(solution)/shard_map/jit(cholesky)/cholesky | solution.py:69
  260.4 9.8 %custom-call.26 = f32[1,128,128]{1,2,0:T(8,128)S(1)} custom-call(f32[1,128,128]{2,1,0:T(8,128)S(1)} %get-tuple-element.190), custom_call_target="InvertDiagBlocksLowerTriangular" | custom-call | tf_op jit(solution)/shard_map/jit(cholesky)/cholesky | solution.py:69
  270.9 11.7 %cholesky.357 = f32[128,128]{1,0:T(8,128)S(1)} custom-call(f32[128,128]{1,0:T(8,128)S(1)} %convolution_subtract_fusion.13), custom_call_target="Cholesky" | custom-call | tf_op jit(solution)/shard_map/jit(cholesky)/cholesky | solution.py:69
  285.8 4.1 while.13
  289.9 19.7 %custom-call.14 = f32[2,128,128]{1,2,0:T(8,128)S(1)} custom-call(f32[2,128,128]{2,1,0:T(8,128)S(1)} %get-tuple-element.24), custom_call_target="InvertDiagBlocksLowerTriangular" | custom-call | tf_op jit(solution)/shard_map/triangular_solve | solution.py:70
  314.5 11.7 %cholesky.374 = f32[128,128]{1,0:T(8,128)S(1)} custom-call(f32[128,128]{1,0:T(8,128)S(1)} %cholesky.577), custom_call_target="Cholesky" | custom-call | tf_op jit(solution)/shard_map/jit(cholesky)/cholesky | solution.py:90
  326.2 9.8 %custom-call.27 = f32[1,128,128]{1,2,0:T(8,128)S(1)} custom-call(f32[1,128,128]{2,1,0:T(8,128)S(1)} %get-tuple-element.186), custom_call_target="InvertDiagBlocksLowerTriangular" | custom-call | tf_op jit(solution)/shard_map/jit(cholesky)/cholesky | solution.py:90
  336.8 12.1 %cholesky.391 = f32[128,128]{1,0:T(8,128)S(1)} custom-call(f32[128,128]{1,0:T(8,128)S(1)} %convolution_subtract_fusion.12), custom_call_target="Cholesky" | custom-call | tf_op jit(solution)/shard_map/jit(cholesky)/cholesky | solution.py:90
  351.7 1.6 collective-permute-start.1
  353.3 4.1 while.14
  357.4 19.7 %custom-call.28 = f32[2,128,128]{1,2,0:T(8,128)S(1)} custom-call(f32[2,128,128]{2,1,0:T(8,128)S(1)} %get-tuple-element.55), custom_call_target="InvertDiagBlocksLowerTriangular" | custom-call | tf_op jit(solution)/shard_map/triangular_solve/custom-call.4 | solution.py:91
  381.2 11.7 %cholesky.408 = f32[128,128]{1,0:T(8,128)S(1)} custom-call(f32[128,128]{1,0:T(8,128)S(1)} %cholesky.580), custom_call_target="Cholesky" | custom-call | tf_op jit(solution)/shard_map/jit(cholesky)/cholesky | solution.py:90
  392.9 9.8 %custom-call.29 = f32[1,128,128]{1,2,0:T(8,128)S(1)} custom-call(f32[1,128,128]{2,1,0:T(8,128)S(1)} %get-tuple-element.182), custom_call_target="InvertDiagBlocksLowerTriangular" | custom-call | tf_op jit(solution)/shard_map/jit(cholesky)/cholesky | solution.py:90
  403.5 11.9 %cholesky.425 = f32[128,128]{1,0:T(8,128)S(1)} custom-call(f32[128,128]{1,0:T(8,128)S(1)} %convolution_subtract_fusion.11), custom_call_target="Cholesky" | custom-call | tf_op jit(solution)/shard_map/jit(cholesky)/cholesky | solution.py:90
  418.1 2.6 collective-permute-start.2
  420.7 4.1 while.15
  424.8 19.7 %custom-call.30 = f32[2,128,128]{1,2,0:T(8,128)S(1)} custom-call(f32[2,128,128]{2,1,0:T(8,128)S(1)} %get-tuple-element.56), custom_call_target="InvertDiagBlocksLowerTriangular" | custom-call | tf_op jit(solution)/shard_map/triangular_solve/custom-call.4 | solution.py:91
  448.6 11.7 %cholesky.442 = f32[128,128]{1,0:T(8,128)S(1)} custom-call(f32[128,128]{1,0:T(8,128)S(1)} %cholesky.583), custom_call_target="Cholesky" | custom-call | tf_op jit(solution)/shard_map/jit(cholesky)/cholesky | solution.py:90
  460.3 9.8 %custom-call.31 = f32[1,128,128]{1,2,0:T(8,128)S(1)} custom-call(f32[1,128,128]{2,1,0:T(8,128)S(1)} %get-tuple-element.178), custom_call_target="InvertDiagBlocksLowerTriangular" | custom-call | tf_op jit(solution)/shard_map/jit(cholesky)/cholesky | solution.py:90
  470.9 12.1 %cholesky.459 = f32[128,128]{1,0:T(8,128)S(1)} custom-call(f32[128,128]{1,0:T(8,128)S(1)} %convolution_subtract_fusion.10), custom_call_target="Cholesky" | custom-call | tf_op jit(solution)/shard_map/jit(cholesky)/cholesky | solution.py:90
  485.5 3.1 collective-permute-start.3
  488.6 3.8 while.16
  492.4 19.7 %custom-call.32 = f32[2,128,128]{1,2,0:T(8,128)S(1)} custom-call(f32[2,128,128]{2,1,0:T(8,128)S(1)} %get-tuple-element.57), custom_call_target="InvertDiagBlocksLowerTriangular" | custom-call | tf_op jit(solution)/shard_map/triangular_solve/custom-call.4 | solution.py:91
  516.2 11.7 %cholesky.476 = f32[128,128]{1,0:T(8,128)S(1)} custom-call(f32[128,128]{1,0:T(8,128)S(1)} %cholesky.586), custom_call_target="Cholesky" | custom-call | tf_op jit(solution)/shard_map/jit(cholesky)/cholesky | solution.py:90
  528.0 9.8 %custom-call.33 = f32[1,128,128]{1,2,0:T(8,128)S(1)} custom-call(f32[1,128,128]{2,1,0:T(8,128)S(1)} %get-tuple-element.174), custom_call_target="InvertDiagBlocksLowerTriangular" | custom-call | tf_op jit(solution)/shard_map/jit(cholesky)/cholesky | solution.py:90
  538.5 11.8 %cholesky.493 = f32[128,128]{1,0:T(8,128)S(1)} custom-call(f32[128,128]{1,0:T(8,128)S(1)} %convolution_subtract_fusion.9), custom_call_target="Cholesky" | custom-call | tf_op jit(solution)/shard_map/jit(cholesky)/cholesky | solution.py:90
  553.9 3.9 while.17
  557.8 19.7 %custom-call.34 = f32[2,128,128]{1,2,0:T(8,128)S(1)} custom-call(f32[2,128,128]{2,1,0:T(8,128)S(1)} %get-tuple-element.58), custom_call_target="InvertDiagBlocksLowerTriangular" | custom-call | tf_op jit(solution)/shard_map/triangular_solve/custom-call.4 | solution.py:91
  581.6 11.7 %cholesky.510 = f32[128,128]{1,0:T(8,128)S(1)} custom-call(f32[128,128]{1,0:T(8,128)S(1)} %cholesky.589), custom_call_target="Cholesky" | custom-call | tf_op jit(solution)/shard_map/jit(cholesky)/cholesky | solution.py:90
  593.3 9.8 %custom-call.35 = f32[1,128,128]{1,2,0:T(8,128)S(1)} custom-call(f32[1,128,128]{2,1,0:T(8,128)S(1)} %get-tuple-element.170), custom_call_target="InvertDiagBlocksLowerTriangular" | custom-call | tf_op jit(solution)/shard_map/jit(cholesky)/cholesky | solution.py:90
  603.9 11.9 %cholesky.527 = f32[128,128]{1,0:T(8,128)S(1)} custom-call(f32[128,128]{1,0:T(8,128)S(1)} %convolution_subtract_fusion.8), custom_call_target="Cholesky" | custom-call | tf_op jit(solution)/shard_map/jit(cholesky)/cholesky | solution.py:90
  619.8 4.1 while.18
  620.4 1.4 bitcast_dynamic-update-slice_fusion.19
  622.5 1.4 bitcast_dynamic-update-slice_fusion.19
  623.9 19.7 %custom-call.36 = f32[2,128,128]{1,2,0:T(8,128)S(1)} custom-call(f32[2,128,128]{2,1,0:T(8,128)S(1)} %get-tuple-element.59), custom_call_target="InvertDiagBlocksLowerTriangular" | custom-call | tf_op jit(solution)/shard_map/triangular_solve/custom-call.4 | solution.py:91
  647.7 11.7 %cholesky.544 = f32[128,128]{1,0:T(8,128)S(1)} custom-call(f32[128,128]{1,0:T(8,128)S(1)} %cholesky.592), custom_call_target="Cholesky" | custom-call | tf_op jit(solution)/shard_map/jit(cholesky)/cholesky | solution.py:90
  659.5 9.8 %custom-call.37 = f32[1,128,128]{1,2,0:T(8,128)S(1)} custom-call(f32[1,128,128]{2,1,0:T(8,128)S(1)} %get-tuple-element.166), custom_call_target="InvertDiagBlocksLowerTriangular" | custom-call | tf_op jit(solution)/shard_map/jit(cholesky)/cholesky | solution.py:90
  669.8 11.9 %cholesky.561 = f32[128,128]{1,0:T(8,128)S(1)} custom-call(f32[128,128]{1,0:T(8,128)S(1)} %convolution_subtract_fusion.7), custom_call_target="Cholesky" | custom-call | tf_op jit(solution)/shard_map/jit(cholesky)/cholesky | solution.py:90
  684.4 4.0 while.19
  688.3 19.7 %custom-call.38 = f32[2,128,128]{1,2,0:T(8,128)S(1)} custom-call(f32[2,128,128]{2,1,0:T(8,128)S(1)} %get-tuple-element.60), custom_call_target="InvertDiagBlocksLowerTriangular" | custom-call | tf_op jit(solution)/shard_map/triangular_solve/custom-call.4 | solution.py:91
  710.1 3.5 copy.87
  (256 shorter events, 78.9 us)
Async XLA Ops:
  7.2 24.8 %copy-start.5 = (f32[64,1024]{1,0:T(8,128)S(1)}, f32[64,1024]{1,0:T(8,128)}, u32[]{:S(2)}) copy-start(f32[64,1024]{1,0:T(8,128)} %param.10) | copy-start | bytes 786436
  18.9 27.4 %copy-start.2 = (f32[256,1024]{1,0:T(8,128)S(1)}, f32[256,1024]{1,0:T(8,128)}, u32[]{:S(2)}) copy-start(f32[256,1024]{1,0:T(8,128)} %param.12) | copy-start | bytes 3145732
  19.8 19.7 %all-to-all-start.1 = ((f32[1,64,16]{2,0,1:T(1,128)}), f32[1,64,16]{2,0,1:T(1,128)S(1)}, u32[]{:S(2)}, u32[]{:S(2)}) async-start(f32[1,64,16]{2,0,1:T(1,128)} %copy.69), calls=%async_computation.1 | async-start | bytes 65536 | tf_op jit(solution)/shard_map/all_to_all | solution.py:46
  39.5 18.4 %all-to-all-start.3 = ((f32[64,1,1024]{2,1,0:T(1,128)}), f32[64,1,1024]{2,1,0:T(1,128)S(1)}, u32[]{:S(2)}, u32[]{:S(2)}) async-start(f32[64,1,1024]{2,1,0:T(1,128)} %reshape.311), calls=%async_computation.3 | async-start | bytes 524288 | tf_op jit(solution)/shard_map/all_to_all | solution.py:43
  57.9 33.1 %all-to-all-start.2 = ((f32[256,64,16]{0,2,1:T(8,128)}), f32[256,64,16]{0,2,1:T(8,128)S(1)}, u32[]{:S(2)}, u32[]{:S(2)}) async-start(f32[256,64,16]{0,2,1:T(8,128)} %bitcast.5), calls=%async_computation.2 | async-start | bytes 2097152 | tf_op jit(solution)/shard_map/all_to_all | solution.py:45
  64.4 75.9 %all-gather.7.cloned.1.call-start = ((), (), s32[]{:S(2)}) async-start(), calls=%async_computation.6 | async-start | bytes 2621440 | tf_op jit(solution)/shard_map/all_gather | solution.py:53
  74.9 87.9 %all-gather.5.cloned.1.call-start = ((), (), s32[]{:S(2)}) async-start(), calls=%async_computation.5 | async-start | bytes 5242880 | tf_op jit(solution)/shard_map/all_gather | solution.py:55
  91.0 4.7 copy-start.3
  96.1 13.2 %copy-start.1 = (f32[1024,64]{1,0:T(8,128)S(1)}, f32[1024,64]{1,0:T(8,128)}, u32[]{:S(2)}) copy-start(f32[1024,64]{1,0:T(8,128)} %gather_fusion.6) | copy-start | bytes 786436
  100.8 34.8 %all-to-all-start = ((f32[256,64,16]{0,2,1:T(8,128)}), f32[256,64,16]{0,2,1:T(8,128)S(1)}, u32[]{:S(2)}, u32[]{:S(2)}) async-start(f32[256,64,16]{0,2,1:T(8,128)} %bitcast.1), calls=%async_computation | async-start | bytes 2097152 | tf_op jit(solution)/shard_map/all_to_all | solution.py:44
  108.9 137.6 %all-reduce.3.cloned.1.call-start = ((), (), s32[]{:S(2)}) async-start(), calls=%async_computation.4 | async-start | bytes 524288 | tf_op jit(solution)/shard_map/psum | solution.py:68
  140.3 2.4 copy-start
  142.7 20.1 %copy-start.4 = (f32[1024,256]{0,1:T(8,128)S(1)}, f32[1024,256]{0,1:T(8,128)}, u32[]{:S(2)}) copy-start(f32[1024,256]{0,1:T(8,128)} %copy.70) | copy-start | bytes 3145732
  285.4 27.1 %collective-permute-start = (f32[256,256]{0,1:T(8,128)S(1)}, f32[256,256]{0,1:T(8,128)S(1)}, u32[]{:S(2)}, u32[]{:S(2)}) collective-permute-start(f32[256,256]{0,1:T(8,128)S(1)} %get-tuple-element.161), channel_id=1, source_target_pairs={{0,4},{4,0},{8,12},{12,8},{16,20},{20,16},{24,28},{28,24},{32,36},... | collective-permute-start | bytes 786440 | tf_op jit(solution)/shard_map/ppermute | solution.py:16
  351.7 27.5 %collective-permute-start.1 = (f32[256,256]{0,1:T(8,128)S(1)}, f32[256,256]{0,1:T(8,128)S(1)}, u32[]{:S(2)}, u32[]{:S(2)}) collective-permute-start(f32[256,256]{0,1:T(8,128)S(1)} %get-tuple-element.159), channel_id=1, source_target_pairs={{0,8},{8,0},{4,12},{12,4},{16,24},{24,16},{20,28},{28,20},{32,40},... | collective-permute-start | bytes 786440 | tf_op jit(solution)/shard_map/ppermute | solution.py:16
  418.1 28.5 %collective-permute-start.2 = (f32[256,256]{0,1:T(8,128)S(1)}, f32[256,256]{0,1:T(8,128)S(1)}, u32[]{:S(2)}, u32[]{:S(2)}) collective-permute-start(f32[256,256]{0,1:T(8,128)S(1)} %get-tuple-element.157), channel_id=1, source_target_pairs={{0,16},{16,0},{4,20},{20,4},{8,24},{24,8},{12,28},{28,12},{32,48},... | collective-permute-start | bytes 786440 | tf_op jit(solution)/shard_map/ppermute | solution.py:16
  485.5 28.7 %collective-permute-start.3 = (f32[256,256]{0,1:T(8,128)S(1)}, f32[256,256]{0,1:T(8,128)S(1)}, u32[]{:S(2)}, u32[]{:S(2)}) collective-permute-start(f32[256,256]{0,1:T(8,128)S(1)} %get-tuple-element.155), channel_id=1, source_target_pairs={{0,32},{32,0},{4,36},{36,4},{8,40},{40,8},{12,44},{44,12},{16,48},... | collective-permute-start | bytes 786440 | tf_op jit(solution)/shard_map/ppermute | solution.py:16
  553.0 26.6 %collective-permute-start.4 = (f32[256,256]{0,1:T(8,128)S(1)}, f32[256,256]{0,1:T(8,128)S(1)}, u32[]{:S(2)}, u32[]{:S(2)}) collective-permute-start(f32[256,256]{0,1:T(8,128)S(1)} %get-tuple-element.153), channel_id=1, source_target_pairs={{0,64},{64,0},{4,68},{68,4},{8,72},{72,8},{12,76},{76,12},{16,80},... | collective-permute-start | bytes 786440 | tf_op jit(solution)/shard_map/ppermute | solution.py:16
  618.5 27.2 %collective-permute-start.5 = (f32[256,256]{0,1:T(8,128)S(1)}, f32[256,256]{0,1:T(8,128)S(1)}, u32[]{:S(2)}, u32[]{:S(2)}) collective-permute-start(f32[256,256]{0,1:T(8,128)S(1)} %get-tuple-element.151), channel_id=1, source_target_pairs={{0,128},{128,0},{4,132},{132,4},{8,136},{136,8},{12,140},{140,12},... | collective-permute-start | bytes 786440 | tf_op jit(solution)/shard_map/ppermute | solution.py:16
Sparse Core Ops, SparseCore 0:
  75.1 34.4 all-gather.6
  111.9 50.8 all-gather.4
  199.3 47.1 all-reduce.2
where the time goes:
time: 730 us; the launch traced here: 721 us
  other arithmetic  404 us (55%)
  waiting for transfers between devices  104 us (14%)
  local copies, waits for them, and re-layouts  75.5 us (10%)
  matrix products  69 us (9%)
  starting transfers between devices  43.8 us (6%)
  between operations  24.6 us (3%)
    another operation x42, other arithmetic, per_device(): merge_lower = jnp.linalg.cholesky(merge_gram)  209 us
    another operation x7, other arithmetic, per_device(): lax.linalg.triangular_solve(merge_lower, jnp.transpose(stacked), left_sid...  118 us
    psum x1, waiting for transfers between devices, per_device(): gram = lax.psum(local_gram, 'blk')  47.3 us
    another operation x7, other arithmetic, per_device(): lower = jnp.linalg.cholesky(gram)  34.7 us
    dot_general x1, matrix products, per_device(): jnp.dot(lax.all_gather(tree_omega, 'blk', axis=1, tiled=True), kernel, pr...  34.6 us
    all_to_all x1, waiting for transfers between devices, per_device(): lax.all_to_all(sketch[:, sending], 'leaf', split_axis=1, concat_axis=1, t...  26 us
    another operation x36, local copies, waits for them, and re-layouts, per_device(): lax.linalg.triangular_solve(merge_lower, jnp.transpose(stacked), left_sid...  23.6 us
    another operation x2, other arithmetic, per_device(): lax.linalg.triangular_solve(lower, off_sketch, left_side=True, lower=True)  19.7 us
  transfers between devices with their start and end apart: 13, of which 6 were waited for; matrix products, arithmetic and copies ran while one was open for 29% of the time, Pallas kernels for 0%

commit v1 on v0

--- a/solution.py
+++ b/solution.py
@@ -1,9 +1,209 @@
+import functools
 import math
 
 import jax
 import jax.numpy as jnp
 from jax import lax
+from jax.experimental import pallas as pl
+from jax.experimental.pallas import tpu as pltpu
 from jax.sharding import PartitionSpec as P
+
+NN = (((1,), (0,)), ((), ()))
+NT = (((1,), (1,)), ((), ()))
+TN = (((0,), (0,)), ((), ()))
+f32, bf16 = jnp.float32, jnp.bfloat16
+
+
+def mm(a, b, dims):
+    return lax.dot_general(a, b, dims, preferred_element_type=f32)
+
+
+def halves(x):
+    hi = x.astype(bf16)
+    return hi, (x - hi.astype(f32)).astype(bf16)
+
+
+def thirds(x):
+    hi = x.astype(bf16)
+    rest = x - hi.astype(f32)
+    mid = rest.astype(bf16)
+    return hi, mid, (rest - mid.astype(f32)).astype(bf16)
+
+
+def dot3(a, b, dims):
+    return mm(a[0], b[0], dims) + (mm(a[0], b[1], dims) + mm(a[1], b[0], dims))
+
+
+def dotf(a, b, dims):
+    return dot3(halves(a), halves(b), dims)
+
+
+def pick(x, hot, dims, left):
+    parts = thirds(x)
+    if left:
+        return mm(parts[0], hot, dims) + mm(parts[1], hot, dims) + mm(parts[2], hot, dims)
+    return mm(hot, parts[0], dims) + mm(hot, parts[1], dims) + mm(hot, parts[2], dims)
+
+
+NB = 32
+W = 8
+
+
+def row_of(x, k):
+    return jnp.broadcast_to(x[k:k + 1, :], x.shape)
+
+
+def diag_inverse(a, seg_base, rows):
+    lane = lax.broadcasted_iota(jnp.int32, (NB, 128), 1)
+    b = jnp.where(lane - seg_base == rows, 1.0, 0.0).astype(f32)
+    scale = jnp.zeros((NB, 128), f32)
+    for k0 in range(0, NB, W):
+        cols = [jnp.take_along_axis(a, seg_base + (k0 + i), axis=1, mode="promise_in_bounds") for i in range(W)]
+        ra = [row_of(a, k0 + i) for i in range(W)]
+        rb = [row_of(b, k0 + i) for i in range(W)]
+        mult = []
+        for i in range(W):
+            k = k0 + i
+            pivot = row_of(cols[i], k)
+            root = lax.rsqrt(pivot)
+            scale = jnp.where(rows == k, root, scale)
+            m = jnp.where(rows > k, cols[i] * (root * root), 0.0)
+            mult.append(m)
+            for t in range(i + 1, W):
+                cols[t] = cols[t] - m * row_of(cols[t], k)
+                mt = row_of(m, k0 + t)
+                ra[t] = ra[t] - mt * ra[i]
+                rb[t] = rb[t] - mt * rb[i]
+        for i in range(W):
+            if k0 + W < NB:
+                a = a - mult[i] * ra[i]
+            b = b - mult[i] * rb[i]
+    return b * scale
+
+
+def tri_kernel(n_inv_groups, order_ref, gram_ref, second_ref, rhs_ref, basis_ref, trans_ref,
+               own, sib, panel, inv, fact, finv):
+    groups = 4
+    size = gram_ref.shape[1]
+    steps = size // NB
+    depth = order_ref.shape[0]
+    slots = 2 * depth + 1
+    isub = lax.broadcasted_iota(jnp.int32, (size, size), 0)
+    hot = [jnp.where(isub == order_ref[l:l + 1, :], 1.0, 0.0).astype(bf16) for l in range(depth)]
+    total = [hot[0]]
+    for l in range(1, depth):
+        total.append(mm(total[-1], hot[l], NN).astype(bf16))
+
+    def reorder(g, q):
+        return pick(pick(g, q, NN, True), q, TN, False)
+
+    running = gram_ref[0]
+    own[0] = running
+    for l in range(depth):
+        g = gram_ref[l + 1]
+        sib[l] = g if l == 0 else reorder(g, total[l - 1])
+        running = running + g
+        own[l + 1] = reorder(running, total[l])
+
+    def dense(s):
+        if s <= depth:
+            return own, s
+        return sib, min(s - depth - 1, depth - 1)
+
+    for j in range(steps):
+        for g in range(groups):
+            lo = NB * j
+            pieces = []
+            for t in range(4):
+                ref, at = dense(min(4 * g + t, slots - 1))
+                pieces.append(ref[at, lo:lo + NB, :])
+            panel[g, j] = jnp.concatenate(pieces, axis=0).T
+
+    lane = lax.broadcasted_iota(jnp.int32, (NB, 128), 1)
+    rows = lax.broadcasted_iota(jnp.int32, (NB, 128), 0)
+    seg_base = (lane // NB) * NB
+    r128 = lax.broadcasted_iota(jnp.int32, (128, 128), 0) // NB
+    l128 = lax.broadcasted_iota(jnp.int32, (128, 128), 1) // NB
+    same = r128 == l128
+
+    def spread(x):
+        return jnp.where(same, jnp.concatenate([x] * 4, axis=0), 0.0)
+
+    for j in range(steps):
+        lo = NB * j
+        nxt = lo + NB
+        for g in range(groups):
+            d = panel[g, j, lo:nxt, :]
+            li = diag_inverse(d, seg_base, rows)
+            lp = dotf(panel[g, j, lo:, :], spread(li), NT)
+            top = jnp.where(lane - seg_base <= rows, lp[:NB], 0.0)
+            if lo:
+                panel[g, j, :lo, :] = jnp.zeros((lo, 128), f32)
+            panel[g, j, lo:nxt, :] = top
+            if nxt < size:
+                panel[g, j, nxt:, :] = lp[NB:]
+                low = lp[NB:]
+                lowh = halves(low)
+                for i in range(j + 1, steps):
+                    at = NB * (i - j - 1)
+                    rhs = halves(spread(low[at:at + NB]))
+                    panel[g, i, NB * i:, :] -= dot3((lowh[0][at:], lowh[1][at:]), rhs, NT)
+            if g < n_inv_groups:
+                lih = halves(li)
+                for c in range(j + 1):
+                    if c == j:
+                        x = li
+                    else:
+                        x = dot3(lih, halves(spread(inv[g, c, lo:nxt, :])), NN)
+                    inv[g, c, lo:nxt, :] = x
+                    if nxt < size:
+                        upd = dot3(lowh, halves(spread(x)), NN)
+                        if c == j:
+                            inv[g, c, nxt:, :] = -upd
+                        else:
+                            inv[g, c, nxt:, :] -= upd
+                if lo:
+                    inv[g, j, :lo, :] = jnp.zeros((lo, 128), f32)
+
+    for j in range(steps):
+        for g in range(groups):
+            flat = panel[g, j].T
+            for t in range(4):
+                if 4 * g + t < slots:
+                    fact[4 * g + t, NB * j:NB * j + NB, :] = flat[NB * t:NB * t + NB]
+            if g < n_inv_groups:
+                flat = inv[g, j].T
+                for t in range(4):
+                    if 4 * g + t <= depth:
+                        finv[4 * g + t, NB * j:NB * j + NB, :] = flat[NB * t:NB * t + NB]
+
+    basis_ref[...] = dotf(finv[0] * math.sqrt(4096), rhs_ref[...], TN)
+    for l in range(depth):
+        v = halves(pick(finv[l + 1] * math.sqrt(2 * size), hot[l], NN, False))
+        second = second_ref[l]
+        trans_ref[l, pl.ds(pl.multiple_of(second * size, size), size), :] = dot3(halves(fact[l]), v, NN)
+        trans_ref[l, pl.ds(pl.multiple_of((1 - second) * size, size), size), :] = dot3(
+            halves(fact[depth + 1 + l]), v, NN)
+
+
+def tri(order, grams, second, rhs):
+    depth, size = order.shape
+    return pl.pallas_call(
+        functools.partial(tri_kernel, 2),
+        out_shape=(jax.ShapeDtypeStruct(rhs.shape, f32), jax.ShapeDtypeStruct((depth, 2 * size, size), f32)),
+        in_specs=[pl.BlockSpec(memory_space=pltpu.VMEM), pl.BlockSpec(memory_space=pltpu.VMEM),
+                  pl.BlockSpec(memory_space=pltpu.SMEM), pl.BlockSpec(memory_space=pltpu.VMEM)],
+        out_specs=[pl.BlockSpec(memory_space=pltpu.VMEM)] * 2,
+        scratch_shapes=[
+            pltpu.VMEM((depth + 1, size, size), f32),
+            pltpu.VMEM((depth, size, size), f32),
+            pltpu.VMEM((4, 8, size, 128), f32),
+            pltpu.VMEM((2, 8, size, 128), f32),
+            pltpu.VMEM((2 * depth + 1, size, size), f32),
+            pltpu.VMEM((depth + 1, size, size), f32),
+        ],
+        compiler_params=pltpu.CompilerParams(vmem_limit_bytes=48 << 20),
+    )(order, grams, second, rhs)
 
 
 def partner(block, axis, stride):
@@ -66,35 +266,16 @@
         preferred_element_type=jnp.float32,
     )
     gram = lax.psum(local_gram, "blk")
-    lower = jnp.linalg.cholesky(gram)
-    basis_t = lax.linalg.triangular_solve(lower, off_sketch, left_side=True, lower=True)
-    leaf_basis = basis_t * math.sqrt(points * blk_count)
-    factor = jnp.transpose(lower)
     leaf_id = lax.axis_index("leaf")
-    depth = leaf_count.bit_length() - 1
-    collected = []
+    depth = column_order.shape[0]
+    grams = [gram]
+    running = gram
     for height in range(depth):
-        sibling = partner(factor, "leaf", height)
-        is_second = leaf_id >> height & 1 == 1
-        upper_half = jnp.where(is_second, sibling, factor)
-        lower_half = jnp.where(is_second, factor, sibling)
-        stacked = jnp.concatenate([upper_half, lower_half], axis=0)
-        stacked = jnp.take(stacked, column_order[height], axis=1)
-        merge_gram = lax.dot_general(
-            stacked,
-            stacked,
-            (((0,), (0,)), ((), ())),
-            precision=lax.Precision.HIGHEST,
-            preferred_element_type=jnp.float32,
-        )
-        merge_lower = jnp.linalg.cholesky(merge_gram)
-        ortho_t = lax.linalg.triangular_solve(
-            merge_lower, jnp.transpose(stacked), left_side=True, lower=True
-        )
-        collected.append(jnp.transpose(ortho_t) * math.sqrt(2 * rank))
-        factor = jnp.transpose(merge_lower)
-    transfers = jnp.stack(collected, axis=0)[None]
-    return (leaf_basis, transfers)
+        grams.append(partner(running, "leaf", height))
+        running = running + grams[-1]
+    second = leaf_id >> jnp.arange(depth, dtype=jnp.int32) & 1
+    leaf_basis, transfers = tri(column_order, jnp.stack(grams), second, off_sketch)
+    return (leaf_basis, transfers[None])
 
 
 def solution(mesh):

time: 730 us -> 349 us (0.48)
  other arithmetic: 404 us -> 14.6 us
  waiting for transfers between devices: 104 us -> 151 us
  local copies, waits for them, and re-layouts: 75.5 us -> 33.8 us
  Pallas kernels: 0 us -> 30.9 us
  matrix products: 69 us -> 51.8 us
  between operations: 24.6 us -> 14.2 us
    another operation x59 -> x0, other arithmetic: 382 us -> none  [the longest x42 209 us: per_device(): merge_lower = jnp.linalg.cholesky(merge_gram)]
    ppermute x6, waiting for transfers between devices: 0.02 us -> 47.5 us  [partner(): return lax.ppermute(block, axis, route)]
    pallas_call x0 -> x1, Pallas kernels: none -> 30.9 us  [tri(): pl.pallas_call(functools.partial(tri_kernel, 2), out_shape=(jax.ShapeDtyp...]
    another operation x69 -> x1, local copies, waits for them, and re-layouts: 28.5 us -> 0.02 us  [per_device(): jnp.stack(grams)]
    another operation x35 -> x0, matrix products: 13 us -> none  [the longest x18 7.26 us: per_device(): lax.linalg.triangular_solve(merge_lower, jnp.transpose(stacked), left_sid...]
  transfers between devices with their start and end apart: 13 -> 13, of which waited for: 6 -> 12; matrix products, arithmetic and copies ran while one was open for 29% -> 15% of each run, Pallas kernels for 0% -> 0%
where the time goes in v1:
time: 349 us; the launch traced here: 342 us
  waiting for transfers between devices  151 us (43%)
  matrix products  51.8 us (15%)
  starting transfers between devices  45.6 us (13%)
  local copies, waits for them, and re-layouts  33.8 us (10%)
  Pallas kernels  30.9 us (9%)
  other arithmetic  14.6 us (4%)
  between operations  14.2 us (4%)
    ppermute x6, waiting for transfers between devices, partner(): return lax.ppermute(block, axis, route)  47.5 us
    psum x1, waiting for transfers between devices, per_device(): gram = lax.psum(local_gram, 'blk')  47.3 us
    dot_general x1, matrix products, per_device(): jnp.dot(lax.all_gather(tree_omega, 'blk', axis=1, tiled=True), kernel, pr...  34.1 us
    pallas_call x1, Pallas kernels, tri(): pl.pallas_call(functools.partial(tri_kernel, 2), out_shape=(jax.ShapeDtyp...  30.9 us
    all_to_all x1, waiting for transfers between devices, per_device(): lax.all_to_all(sketch[:, sending], 'leaf', split_axis=1, concat_axis=1, t...  26.2 us
    all_to_all x1, waiting for transfers between devices, per_device(): lax.all_to_all(omega[:, sending], 'leaf', split_axis=1, concat_axis=1, ti...  16 us
    dot_general x1, matrix products, kernel_block(): lax.dot_general(row_feat, col_feat, (((0,), (0,)), ((), ())), precision=l...  16 us
    all_to_all x1, starting transfers between devices, per_device(): lax.all_to_all(position_row, 'leaf', split_axis=1, concat_axis=1, tiled=T...  12.2 us
  transfers between devices with their start and end apart: 13, of which 12 were waited for; matrix products, arithmetic and copies ran while one was open for 15% of the time, Pallas kernels for 0%

profile of v1, /device:TPU:6, one launch (start us, length us, event | category | flops | bytes accessed | tf_op | source)
XLA Modules:
  0.0 342.0 jit_solution(17655067495941470193)
XLA Ops:
  7.2 0.0 copy-start.1
  7.2 5.1 %sort.31 = (s32[1024]{0:T(1024)}, s32[1024]{0:T(1024)S(1)}) sort(s32[1024]{0:T(1024)} %param.8, s32[1024]{0:T(1024)S(1)} %iota.10), dimensions={0}, to_apply=%region_0.0 | sort | flops 10240 | bytes 16384 | tf_op jit(solution)/shard_map/jit(argsort)/sort | solution.py:239
  12.3 0.0 copy-done.1
  12.3 0.0 copy-start.8
  12.3 4.5 %gather_fusion.1 = s32[1024]{0:T(1024)S(1)} fusion(s32[1024]{0:T(1024)S(1)} %copy-done.1, s32[1024]{0:T(1024)S(1)} %fusion.15), kind=kCustom, calls=%fused_computation.1 | custom fusion | bytes 12288 | tf_op jit(solution)/shard_map/gather | solution.py:240
  16.9 0.1 gather.25
  16.9 0.1 copy.21
  17.0 0.7 copy.24
  17.7 12.2 %all-to-all-start.1 = ((f32[1,64,16]{2,0,1:T(1,128)}), f32[1,64,16]{2,0,1:T(1,128)S(1)}, u32[]{:S(2)}, u32[]{:S(2)}) async-start(f32[1,64,16]{2,0,1:T(1,128)} %copy.24), calls=%async_computation.1 | async-start | bytes 65536 | tf_op jit(solution)/shard_map/all_to_all | solution.py:246
  29.9 0.0 copy-done.8
  29.9 0.0 copy-start.5
  29.9 0.2 copy.27
  30.1 2.8 gather_fusion.5
  32.9 1.0 reshape.144
  34.0 3.4 %all-to-all-done.1 = f32[1,64,16]{2,0,1:T(1,128)S(1)} async-done(((f32[1,64,16]{2,0,1:T(1,128)}), f32[1,64,16]{2,0,1:T(1,128)S(1)}, u32[]{:S(2)}, u32[]{:S(2)}) %all-to-all-start.1) | async-done | bytes 4128 | tf_op jit(solution)/shard_map/all_to_all | solution.py:246
  37.4 6.9 %all-to-all-start.3 = ((f32[64,1,1024]{2,1,0:T(1,128)}), f32[64,1,1024]{2,1,0:T(1,128)S(1)}, u32[]{:S(2)}, u32[]{:S(2)}) async-start(f32[64,1,1024]{2,1,0:T(1,128)} %reshape.144), calls=%async_computation.3 | async-start | bytes 524288 | tf_op jit(solution)/shard_map/all_to_all | solution.py:243
  44.3 0.3 copy.26
  44.6 4.7 %gather_fusion.3 = f32[1024,256]{1,0:T(8,128)} fusion(f32[256,1024]{0,1:T(8,128)S(1)} %copy.26, s32[1024]{0:T(1024)S(1)} %fusion.15), kind=kCustom, calls=%fused_computation.3 | custom fusion | bytes 2101248 | tf_op jit(solution)/shard_map/gather | solution.py:245
  49.3 6.5 %all-to-all-done.3 = f32[64,1,1024]{2,1,0:T(1,128)S(1)} async-done(((f32[64,1,1024]{2,1,0:T(1,128)}), f32[64,1,1024]{2,1,0:T(1,128)S(1)}, u32[]{:S(2)}, u32[]{:S(2)}) %all-to-all-start.3) | async-done | bytes 262176 | tf_op jit(solution)/shard_map/all_to_all | solution.py:243
  55.9 6.5 %all-to-all-start.2 = ((f32[256,64,16]{0,2,1:T(8,128)}), f32[256,64,16]{0,2,1:T(8,128)S(1)}, u32[]{:S(2)}, u32[]{:S(2)}) async-start(f32[256,64,16]{0,2,1:T(8,128)} %bitcast.5), calls=%async_computation.2 | async-start | bytes 2097152 | tf_op jit(solution)/shard_map/all_to_all | solution.py:245
  62.3 0.0 all-gather.7.cloned.1.call-start
  62.4 0.1 convert_reduce_fusion
  62.5 0.1 convert_element_type.19
  62.6 4.4 %sort.32 = (s32[1024]{0:T(1024)}, s32[1024]{0:T(1024)S(1)}) sort(s32[1024]{0:T(1024)S(1)} %convert_element_type.19, s32[1024]{0:T(1024)S(1)} %iota.11), dimensions={0}, to_apply=%region_1.2 | sort | flops 10240 | bytes 16384 | tf_op jit(solution)/shard_map/jit(argsort)/sort | solution.py:249
  66.9 0.5 broadcast.86
  67.5 1.3 reduce.4
  68.7 0.1 reshape.145
  68.9 4.0 %gather_fusion.6 = f32[1024,64]{1,0:T(8,128)} fusion(f32[64,1024]{0,1:T(8,128)S(1)} %bitcast.41, s32[1024]{0:T(1024)S(1)} %fusion.16), kind=kCustom, calls=%fused_computation.6 | custom fusion | bytes 528384 | tf_op jit(solution)/shard_map/gather | solution.py:250
  72.9 0.0 all-gather.7.cloned.1.call-update
  72.9 0.0 all-gather.5.cloned.1.call-start
  73.0 16.0 %all-to-all-done.2 = f32[256,64,16]{0,2,1:T(8,128)S(1)} async-done(((f32[256,64,16]{0,2,1:T(8,128)}), f32[256,64,16]{0,2,1:T(8,128)S(1)}, u32[]{:S(2)}, u32[]{:S(2)}) %all-to-all-start.2) | async-done | bytes 1048608 | tf_op jit(solution)/shard_map/all_to_all | solution.py:245
  89.0 4.7 %gather_fusion.4 = f32[1024,256]{1,0:T(8,128)} fusion(f32[256,1024]{0,1:T(8,128)S(1)} %bitcast.39, s32[1024]{0:T(1024)S(1)} %fusion.16), kind=kCustom, calls=%fused_computation.4 | custom fusion | bytes 2101248 | tf_op jit(solution)/shard_map/gather | solution.py:252
  93.7 0.0 all-gather.5.cloned.1.call-update
  93.7 0.3 copy.20
  94.0 4.7 %gather_fusion = f32[1024,256]{1,0:T(8,128)} fusion(f32[256,1024]{0,1:T(8,128)S(1)} %copy.20, s32[1024]{0:T(1024)S(1)} %fusion.15), kind=kCustom, calls=%fused_computation | custom fusion | bytes 2101248 | tf_op jit(solution)/shard_map/gather | solution.py:244
  98.7 8.2 %all-to-all-start = ((f32[256,64,16]{0,2,1:T(8,128)}), f32[256,64,16]{0,2,1:T(8,128)S(1)}, u32[]{:S(2)}, u32[]{:S(2)}) async-start(f32[256,64,16]{0,2,1:T(8,128)} %bitcast.1), calls=%async_computation | async-start | bytes 2097152 | tf_op jit(solution)/shard_map/all_to_all | solution.py:244
  107.0 0.2 all-reduce.2.cloned.1.call-start
  107.2 0.2 multiply_reduce_fusion.1
  107.4 26.2 %all-to-all-done = f32[256,64,16]{0,2,1:T(8,128)S(1)} async-done(((f32[256,64,16]{0,2,1:T(8,128)}), f32[256,64,16]{0,2,1:T(8,128)S(1)}, u32[]{:S(2)}, u32[]{:S(2)}) %all-to-all-start) | async-done | bytes 1048608 | tf_op jit(solution)/shard_map/all_to_all | solution.py:244
  133.6 3.5 %gather_fusion.2 = f32[1024,256]{1,0:T(8,128)S(1)} fusion(f32[256,1024]{0,1:T(8,128)S(1)} %bitcast.40, s32[1024]{0:T(1024)S(1)} %fusion.16), kind=kCustom, calls=%fused_computation.2 | custom fusion | bytes 2101248 | tf_op jit(solution)/shard_map/gather | solution.py:251
  137.1 1.3 copy.25
  138.4 2.4 multiply_reduce_fusion
  140.8 0.0 copy-start.7
  140.8 16.0 %fusion.19 = f32[4096,1024]{1,0:T(8,128)} fusion(f32[64,4096]{0,1:T(8,128)S(1)} %copy-done.2, f32[1024,64]{1,0:T(8,128)S(1)} %copy-done.3), kind=kOutput, calls=%fused_computation.40 | convolution fusion | flops 3221225472 | bytes 18087936 | tf_op jit(solution)/shard_map/dot_general | solution.py:221
  156.8 4.0 %all-gather.5.cloned.1.call-done = f32[256,4096]{0,1:T(8,128)} async-done(((f32[256,1024]{0,1:T(8,128)}), f32[256,4096]{0,1:T(8,128)}) %all-gather.5.cloned.1.call-update) | async-done | bytes 4194320 | tf_op jit(solution)/shard_map/all_gather | solution.py:255
  160.8 34.1 %fusion.10.rhs_ref = f32[256,1024]{1,0:T(8,128)S(1)} fusion(f32[256,4096]{0,1:T(8,128)} %all-gather.5.cloned.1.call-done, f32[4096,1024]{1,0:T(8,128)} %fusion.19, f32[1024]{0:T(1024)S(1)} %multiply_reduce_fusion.1, f32[4096]{0:T(1024)S(1)} %multiply_reduce_fusion, f32[1024,256]{0,1:T(8,128)S(1)} %copy-done.7), kind=kOutput, calls=%fused_computation.18 | convolution fusion | flops 12901941248 | bytes 23089152 | tf_op jit(solution)/shard_map/dot_general | solution.py:254
  194.9 1.7 fusion.20
  196.7 0.0 all-reduce.2.cloned.1.call-update
  196.7 47.3 %all-reduce.2.cloned.1.call-done = f32[256,256]{1,0:T(8,128)} async-done(((f32[256,256]{1,0:T(8,128)}), f32[256,256]{1,0:T(8,128)}) %all-reduce.2.cloned.1.call-update) | async-done | bytes 262160 | tf_op jit(solution)/shard_map/psum | solution.py:268
  244.0 0.0 collective-permute-start
  244.0 1.7 collective-permute-done
  245.7 1.0 add.61
  246.7 1.6 collective-permute-start.1
  248.4 6.8 %collective-permute-done.1 = f32[256,256]{1,0:T(8,128)S(1)} collective-permute-done((f32[256,256]{1,0:T(8,128)S(1)}, f32[256,256]{1,0:T(8,128)S(1)}, u32[]{:S(2)}, u32[]{:S(2)}) %collective-permute-start.1) | collective-permute-done | bytes 262176 | tf_op jit(solution)/shard_map/ppermute | solution.py:216
  255.2 2.6 collective-permute-start.2
  257.8 11.5 %collective-permute-done.2 = f32[256,256]{1,0:T(8,128)S(1)} collective-permute-done((f32[256,256]{1,0:T(8,128)S(1)}, f32[256,256]{1,0:T(8,128)S(1)}, u32[]{:S(2)}, u32[]{:S(2)}) %collective-permute-start.2) | collective-permute-done | bytes 262176 | tf_op jit(solution)/shard_map/ppermute | solution.py:216
  269.4 5.8 %collective-permute-start.3 = (f32[256,256]{1,0:T(8,128)S(1)}, f32[256,256]{1,0:T(8,128)S(1)}, u32[]{:S(2)}, u32[]{:S(2)}) collective-permute-start(f32[256,256]{1,0:T(8,128)S(1)} %add.63), channel_id=1, source_target_pairs={{0,32},{32,0},{4,36},{36,4},{8,40},{40,8},{12,44},{44,12},{16,48},... | collective-permute-start | bytes 786440 | tf_op jit(solution)/shard_map/ppermute | solution.py:216
  275.2 0.0 copy-start
  275.3 12.0 %collective-permute-done.3 = f32[256,256]{1,0:T(8,128)S(1)} collective-permute-done((f32[256,256]{1,0:T(8,128)S(1)}, f32[256,256]{1,0:T(8,128)S(1)}, u32[]{:S(2)}, u32[]{:S(2)}) %collective-permute-start.3) | collective-permute-done | bytes 262176 | tf_op jit(solution)/shard_map/ppermute | solution.py:216
  287.3 0.9 collective-permute-start.4
  288.3 7.7 %collective-permute-done.4 = f32[256,256]{1,0:T(8,128)S(1)} collective-permute-done((f32[256,256]{1,0:T(8,128)S(1)}, f32[256,256]{1,0:T(8,128)S(1)}, u32[]{:S(2)}, u32[]{:S(2)}) %collective-permute-start.4) | collective-permute-done | bytes 262176 | tf_op jit(solution)/shard_map/ppermute | solution.py:216
  296.0 0.6 collective-permute-start.5
  296.6 7.8 %collective-permute-done.5 = f32[256,256]{1,0:T(8,128)S(1)} collective-permute-done((f32[256,256]{1,0:T(8,128)S(1)}, f32[256,256]{1,0:T(8,128)S(1)}, u32[]{:S(2)}, u32[]{:S(2)}) %collective-permute-start.5) | collective-permute-done | bytes 262176 | tf_op jit(solution)/shard_map/ppermute | solution.py:216
  304.5 30.9 %shard_map.68 = (f32[256,1024]{1,0:T(8,128)}, f32[6,512,256]{2,1,0:T(8,128)}) custom-call(s32[6,256]{1,0:T(8,128)S(1)} %copy-done, f32[7,256,256]{2,1,0:T(8,128)S(1)} %bitcast_dynamic-update-slice_fusion.gram_ref, s32[6]{0:T(128)S(1)} %shift-right-arithmetic_and_fusion.second_ref, f32[256,1024]{1,0:T(8,128)S(1)} %fusion.10.rhs_ref), custom_call_target="tpu_custom_call" | custom-call | tf_op jit(solution)/shard_map/pallas_call | solution.py:191
  (29 shorter events, 0.3 us)
Async XLA Ops:
  7.2 5.1 %copy-start.1 = (s32[1024]{0:T(1024)S(1)}, s32[1024]{0:T(1024)}, u32[]{:S(2)}) copy-start(s32[1024]{0:T(1024)} %param.8) | copy-start | bytes 12292
  12.3 17.6 %copy-start.8 = (f32[64,1024]{1,0:T(8,128)S(1)}, f32[64,1024]{1,0:T(8,128)}, u32[]{:S(2)}) copy-start(f32[64,1024]{1,0:T(8,128)} %param.5) | copy-start | bytes 786436
  17.7 19.7 %all-to-all-start.1 = ((f32[1,64,16]{2,0,1:T(1,128)}), f32[1,64,16]{2,0,1:T(1,128)S(1)}, u32[]{:S(2)}, u32[]{:S(2)}) async-start(f32[1,64,16]{2,0,1:T(1,128)} %copy.24), calls=%async_computation.1 | async-start | bytes 65536 | tf_op jit(solution)/shard_map/all_to_all | solution.py:246
  29.9 14.4 %copy-start.5 = (f32[256,1024]{1,0:T(8,128)S(1)}, f32[256,1024]{1,0:T(8,128)}, u32[]{:S(2)}) copy-start(f32[256,1024]{1,0:T(8,128)} %param.7) | copy-start | bytes 3145732
  37.4 18.5 %all-to-all-start.3 = ((f32[64,1,1024]{2,1,0:T(1,128)}), f32[64,1,1024]{2,1,0:T(1,128)S(1)}, u32[]{:S(2)}, u32[]{:S(2)}) async-start(f32[64,1,1024]{2,1,0:T(1,128)} %reshape.144), calls=%async_computation.3 | async-start | bytes 524288 | tf_op jit(solution)/shard_map/all_to_all | solution.py:243
  55.9 33.1 %all-to-all-start.2 = ((f32[256,64,16]{0,2,1:T(8,128)}), f32[256,64,16]{0,2,1:T(8,128)S(1)}, u32[]{:S(2)}, u32[]{:S(2)}) async-start(f32[256,64,16]{0,2,1:T(8,128)} %bitcast.5), calls=%async_computation.2 | async-start | bytes 2097152 | tf_op jit(solution)/shard_map/all_to_all | solution.py:245
  62.3 76.1 %all-gather.7.cloned.1.call-start = ((), (), s32[]{:S(2)}) async-start(), calls=%async_computation.6 | async-start | bytes 2621440 | tf_op jit(solution)/shard_map/all_gather | solution.py:253
  72.9 87.9 %all-gather.5.cloned.1.call-start = ((), (), s32[]{:S(2)}) async-start(), calls=%async_computation.5 | async-start | bytes 5242880 | tf_op jit(solution)/shard_map/all_gather | solution.py:255
  89.0 4.7 %copy-start.6 = (f32[256,1024]{1,0:T(8,128)S(1)}, f32[256,1024]{1,0:T(8,128)}, u32[]{:S(2)}) copy-start(f32[256,1024]{1,0:T(8,128)} %param.6) | copy-start | bytes 3145732
  98.7 8.5 %copy-start.3 = (f32[1024,64]{1,0:T(8,128)S(1)}, f32[1024,64]{1,0:T(8,128)}, u32[]{:S(2)}) copy-start(f32[1024,64]{1,0:T(8,128)} %gather_fusion.6) | copy-start | bytes 786436
  98.7 34.9 %all-to-all-start = ((f32[256,64,16]{0,2,1:T(8,128)}), f32[256,64,16]{0,2,1:T(8,128)S(1)}, u32[]{:S(2)}, u32[]{:S(2)}) async-start(f32[256,64,16]{0,2,1:T(8,128)} %bitcast.1), calls=%async_computation | async-start | bytes 2097152 | tf_op jit(solution)/shard_map/all_to_all | solution.py:244
  107.0 137.0 %all-reduce.2.cloned.1.call-start = ((), (), s32[]{:S(2)}) async-start(), calls=%async_computation.4 | async-start | bytes 524288 | tf_op jit(solution)/shard_map/psum | solution.py:268
  138.4 2.4 copy-start.2
  140.8 20.0 %copy-start.7 = (f32[1024,256]{0,1:T(8,128)S(1)}, f32[1024,256]{0,1:T(8,128)}, u32[]{:S(2)}) copy-start(f32[1024,256]{0,1:T(8,128)} %copy.25) | copy-start | bytes 3145732
  244.0 31.2 %copy-start.4 = (f32[256,256]{1,0:T(8,128)S(1)}, f32[256,256]{1,0:T(8,128)}, u32[]{:S(2)}) copy-start(f32[256,256]{1,0:T(8,128)} %all-reduce.2.cloned.1.call-done) | copy-start | bytes 786436
  244.0 1.7 collective-permute-start
  246.7 8.4 %collective-permute-start.1 = (f32[256,256]{1,0:T(8,128)S(1)}, f32[256,256]{1,0:T(8,128)S(1)}, u32[]{:S(2)}, u32[]{:S(2)}) collective-permute-start(f32[256,256]{1,0:T(8,128)S(1)} %add.61), channel_id=1, source_target_pairs={{0,8},{8,0},{4,12},{12,4},{16,24},{24,16},{20,28},{28,20},{32,40},... | collective-permute-start | bytes 786440 | tf_op jit(solution)/shard_map/ppermute | solution.py:216
  255.2 14.1 %collective-permute-start.2 = (f32[256,256]{1,0:T(8,128)S(1)}, f32[256,256]{1,0:T(8,128)S(1)}, u32[]{:S(2)}, u32[]{:S(2)}) collective-permute-start(f32[256,256]{1,0:T(8,128)S(1)} %add.62), channel_id=1, source_target_pairs={{0,16},{16,0},{4,20},{20,4},{8,24},{24,8},{12,28},{28,12},{32,48},... | collective-permute-start | bytes 786440 | tf_op jit(solution)/shard_map/ppermute | solution.py:216
  269.4 17.9 %collective-permute-start.3 = (f32[256,256]{1,0:T(8,128)S(1)}, f32[256,256]{1,0:T(8,128)S(1)}, u32[]{:S(2)}, u32[]{:S(2)}) collective-permute-start(f32[256,256]{1,0:T(8,128)S(1)} %add.63), channel_id=1, source_target_pairs={{0,32},{32,0},{4,36},{36,4},{8,40},{40,8},{12,44},{44,12},{16,48},... | collective-permute-start | bytes 786440 | tf_op jit(solution)/shard_map/ppermute | solution.py:216
  275.2 29.2 %copy-start = (s32[6,256]{1,0:T(8,128)S(1)}, s32[6,256]{1,0:T(8,128)}, u32[]{:S(2)}) copy-start(s32[6,256]{1,0:T(8,128)} %order_ref.1) | copy-start | bytes 18436
  287.3 8.7 %collective-permute-start.4 = (f32[256,256]{1,0:T(8,128)S(1)}, f32[256,256]{1,0:T(8,128)S(1)}, u32[]{:S(2)}, u32[]{:S(2)}) collective-permute-start(f32[256,256]{1,0:T(8,128)S(1)} %add.64), channel_id=1, source_target_pairs={{0,64},{64,0},{4,68},{68,4},{8,72},{72,8},{12,76},{76,12},{16,80},... | collective-permute-start | bytes 786440 | tf_op jit(solution)/shard_map/ppermute | solution.py:216
  296.0 8.4 %collective-permute-start.5 = (f32[256,256]{1,0:T(8,128)S(1)}, f32[256,256]{1,0:T(8,128)S(1)}, u32[]{:S(2)}, u32[]{:S(2)}) collective-permute-start(f32[256,256]{1,0:T(8,128)S(1)} %add.65), channel_id=1, source_target_pairs={{0,128},{128,0},{4,132},{132,4},{8,136},{136,8},{12,140},{140,12},... | collective-permute-start | bytes 786440 | tf_op jit(solution)/shard_map/ppermute | solution.py:216
Sparse Core Ops, SparseCore 0:
  73.0 34.4 all-gather.6
  109.9 50.8 all-gather.4
  196.8 47.1 all-reduce.1

commit v2 on v1

--- a/solution.py
+++ b/solution.py
@@ -84,7 +84,8 @@
 def tri_kernel(n_inv_groups, order_ref, gram_ref, second_ref, rhs_ref, basis_ref, trans_ref,
                own, sib, panel, inv, fact, finv):
     groups = 4
-    size = gram_ref.shape[1]
+    size = order_ref.shape[1]
+    half = size // 2
     steps = size // NB
     depth = order_ref.shape[0]
     slots = 2 * depth + 1
@@ -97,10 +98,15 @@
     def reorder(g, q):
         return pick(pick(g, q, NN, True), q, TN, False)
 
-    running = gram_ref[0]
+    def unfold(at):
+        low = gram_ref[at, half:2 * half, :]
+        top = jnp.concatenate([gram_ref[at, 0:half, :], jnp.transpose(low)], axis=1)
+        return jnp.concatenate([top, jnp.concatenate([low, gram_ref[at, 2 * half:, :]], axis=1)], axis=0)
+
+    running = unfold(0)
     own[0] = running
     for l in range(depth):
-        g = gram_ref[l + 1]
+        g = unfold(l + 1)
         sib[l] = g if l == 0 else reorder(g, total[l - 1])
         running = running + g
         own[l + 1] = reorder(running, total[l])
@@ -177,7 +183,7 @@
                     if 4 * g + t <= depth:
                         finv[4 * g + t, NB * j:NB * j + NB, :] = flat[NB * t:NB * t + NB]
 
-    basis_ref[...] = dotf(finv[0] * math.sqrt(4096), rhs_ref[...], TN)
+    basis_ref[...] = dotf(finv[0] * math.sqrt(rhs_ref.shape[1] * lax.axis_size("blk")), rhs_ref[...], TN)
     for l in range(depth):
         v = halves(pick(finv[l + 1] * math.sqrt(2 * size), hot[l], NN, False))
         second = second_ref[l]
@@ -206,75 +212,316 @@
     )(order, grams, second, rhs)
 
 
-def partner(block, axis, stride):
-    count = lax.axis_size(axis)
-    route = []
-    for low in range(count):
-        high = low | 1 << stride
-        if high != low and high < count:
-            route += [(low, high), (high, low)]
-    return lax.ppermute(block, axis, route)
-
-
-def kernel_block(row_feat, col_feat):
-    width = row_feat.shape[0]
-    inner = lax.dot_general(
-        row_feat,
-        col_feat,
-        (((0,), (0,)), ((), ())),
-        precision=lax.Precision.HIGHEST,
-        preferred_element_type=jnp.float32,
-    )
-    norms_a = jnp.sum(row_feat * row_feat, axis=0)
-    norms_b = jnp.sum(col_feat * col_feat, axis=0)
-    distance = norms_a[:, None] + norms_b[None, :] - 2.0 * inner
-    return jnp.exp(distance * (-2.0 / width))
+MESH = pl.DeviceIdType.MESH
+
+
+def sums_kernel(gram_ref, out_ref, flat, part, run, got, stage, full,
+                part_send, part_recv, got_send, got_recv, fwd_send, fwd_recv):
+    leaf, blk = lax.axis_index("leaf"), lax.axis_index("blk")
+    n_blk = lax.axis_size("blk")
+    rounds = run.shape[0]
+    half = flat.shape[1]
+    piece = run.shape[1]
+
+    def mates(r):
+        unit = 4 ** r
+        digit = (leaf // unit) % 4
+        moved = (digit + 1 - 2 * (digit % 2), digit + 2 - 4 * (digit // 2), 3 - digit)
+        return [leaf + (m - digit) * unit for m in moved]
+
+    barrier = pltpu.get_barrier_semaphore()
+    for d in range(1, n_blk):
+        pl.semaphore_signal(barrier, inc=1, device_id=(leaf, (blk + d) % n_blk), device_id_type=MESH)
+    for r in range(rounds):
+        for mate in mates(r):
+            pl.semaphore_signal(barrier, inc=1, device_id=(mate, blk), device_id_type=MESH)
+    flat[0:half] = gram_ref[0:half, 0:half]
+    flat[half:2 * half] = gram_ref[half:, 0:half]
+    flat[2 * half:] = gram_ref[half:, half:]
+    pl.semaphore_wait(barrier, n_blk - 1 + 3 * rounds)
+
+    started = []
+
+    def send(src, dst, s_sem, r_sem, device):
+        copy = pltpu.make_async_remote_copy(src_ref=src, dst_ref=dst, send_sem=s_sem, recv_sem=r_sem,
+                                            device_id=device, device_id_type=MESH)
+        copy.start()
+        started.append(copy)
+        return copy
+
+    first = []
+    for d in range(1, n_blk):
+        peer = (blk + d) % n_blk
+        first.append(send(flat.at[pl.ds(pl.multiple_of(peer * piece, 8), piece)], part.at[d - 1],
+                          part_send.at[d - 1], part_recv.at[d - 1], (leaf, peer)))
+    for copy in first:
+        copy.wait_recv()
+    mine = pl.multiple_of(blk * piece, 8)
+    run[0] = flat[pl.ds(mine, piece)] + ((part[0] + part[1]) + part[2])
+    stage[0] = run[0]
+    full[0, pl.ds(mine, piece)] = stage[0]
+    forwards = []
+    for r in range(rounds):
+        copies = [send(run.at[r], got.at[r, m], got_send.at[r, m], got_recv.at[r, m], (mate, blk))
+                  for m, mate in enumerate(mates(r))]
+        if r == 0:
+            for d in range(1, n_blk):
+                forwards.append(send(stage.at[0], full.at[0, pl.ds(mine, piece)], fwd_send.at[0, d - 1],
+                                     fwd_recv.at[0, d - 1], (leaf, (blk + d) % n_blk)))
+        for copy in copies:
+            copy.wait_recv()
+        near = got[r, 0]
+        far = got[r, 1] + got[r, 2]
+        if r + 1 < rounds:
+            run[r + 1] = run[r] + near + far
+        for k, value in enumerate((near, far)):
+            at = 1 + 2 * r + k
+            stage[at] = value
+            full[at, pl.ds(mine, piece)] = value
+        for k in range(2):
+            at = 1 + 2 * r + k
+            for d in range(1, n_blk):
+                forwards.append(send(stage.at[at], full.at[at, pl.ds(mine, piece)], fwd_send.at[at, d - 1],
+                                     fwd_recv.at[at, d - 1], (leaf, (blk + d) % n_blk)))
+    for copy in forwards:
+        copy.wait_recv()
+    for copy in started:
+        copy.wait_send()
+    out_ref[...] = full[...]
+
+
+def subtree_sums(gram, depth):
+    size = gram.shape[0]
+    half = size // 2
+    rows = 3 * half
+    n_blk = 4
+    piece = rows // n_blk
+    rounds = depth // 2
+    vm = lambda *shape: pltpu.VMEM(shape, f32)
+    return pl.pallas_call(
+        sums_kernel,
+        out_shape=jax.ShapeDtypeStruct((depth + 1, rows, half), f32),
+        in_specs=[pl.BlockSpec(memory_space=pltpu.VMEM)],
+        out_specs=pl.BlockSpec(memory_space=pltpu.VMEM),
+        scratch_shapes=[
+            vm(rows, half), vm(n_blk - 1, piece, half), vm(rounds, piece, half), vm(rounds, 3, piece, half),
+            vm(depth + 1, piece, half), vm(depth + 1, rows, half),
+            pltpu.SemaphoreType.DMA((n_blk - 1,)), pltpu.SemaphoreType.DMA((n_blk - 1,)),
+            pltpu.SemaphoreType.DMA((rounds, 3)), pltpu.SemaphoreType.DMA((rounds, 3)),
+            pltpu.SemaphoreType.DMA((depth + 1, n_blk - 1)), pltpu.SemaphoreType.DMA((depth + 1, n_blk - 1)),
+        ],
+        compiler_params=pltpu.CompilerParams(collective_id=1, has_side_effects=True, vmem_limit_bytes=16 << 20),
+    )(gram)
+
+
+def near_kernel(dims, slot_ref, feat_ref, sketch_ref, omega_ref, gram_ref, rhs_ref,
+                hot, out_a, out_b, in_a, in_b, side, acc, row_aug,
+                send_a, recv_a, send_b, recv_b, side_send, side_recv):
+    count_x, count_z, count_core = dims
+    count = count_x * count_z * count_core
+    leaf, blk = lax.axis_index("leaf"), lax.axis_index("blk")
+    n_blk = lax.axis_size("blk")
+    points = slot_ref.shape[1]
+    chunk = points // count
+    feats = feat_ref.shape[0]
+    rank = omega_ref.shape[0]
+    tail = out_a.shape[1] - rank
+    groups = 4
+    per = count // groups
+    wide = points // groups
+    my_core = leaf % count_core
+    my_z = (leaf // count_core) % count_z
+    my_x = leaf // (count_core * count_z)
+    right, left = (blk + 1) % n_blk, (blk + n_blk - 1) % n_blk
+
+    def target(t):
+        dz = (t * 3) % count_z
+        a = t // count_z
+        dx = (a + t) % count_x
+        dc = (a // count_x + t) % count_core
+        return (((my_x + dx) % count_x) * count_z + (my_z + dz) % count_z) * count_core + (my_core + dc) % count_core
+
+    barrier = pltpu.get_barrier_semaphore()
+
+    @pl.loop(1, count)
+    def _(t):
+        pl.semaphore_signal(barrier, inc=1, device_id=(target(t), blk), device_id_type=MESH)
+
+    for peer in (right, left):
+        pl.semaphore_signal(barrier, inc=1, device_id=(leaf, peer), device_id_type=MESH)
+
+    own_row = slot_ref[...].astype(f32)
+    own_col = jnp.transpose(jnp.broadcast_to(own_row, (128, points)))
+    for c in range(points // 128):
+        piece = own_row[:, 128 * c:128 * c + 128]
+        place = jnp.sum(jnp.where(own_col < piece, 1.0, 0.0), axis=0, keepdims=True).astype(jnp.int32)
+        at = lax.broadcasted_iota(jnp.int32, (points, 128), 0)
+        hot[:, 128 * c:128 * c + 128] = jnp.where(at == place, 1.0, 0.0).astype(bf16)
+
+    place_row = (slot_ref[...] % points).astype(f32)
+    extra = jnp.concatenate(
+        [feat_ref[...], place_row, jnp.zeros((tail - feats - 1, points), f32)], axis=0)
+    eh, el = halves(extra)
+    oh, ol = halves(omega_ref[...])
+
+    def sort_rows(r, hi, lo):
+        h = hot[pl.ds(pl.multiple_of(r * 128, 128), 128), :]
+        return mm(h, hi, NT) + mm(h, lo, NT)
+
+    for r in range(points // 128):
+        out_a[128 * r:128 * r + 128, 0:rank] = sort_rows(r, oh, ol)
+        out_a[128 * r:128 * r + 128, rank:] = sort_rows(r, eh, el)
+
+    pl.semaphore_wait(barrier, count - 1 + 2)
+
+    def to_leaf(t, out, into, s_sem, r_sem):
+        goal = target(t)
+        return pltpu.make_async_remote_copy(
+            src_ref=out.at[pl.ds(pl.multiple_of(goal * chunk, chunk), chunk)],
+            dst_ref=into.at[pl.ds(pl.multiple_of(t * chunk, chunk), chunk)],
+            send_sem=s_sem.at[t], recv_sem=r_sem.at[t], device_id=(goal, blk), device_id_type=MESH)
+
+    @pl.loop(1, count)
+    def _(t):
+        to_leaf(t, out_a, in_a, send_a, recv_a).start()
+
+    sh, sl = halves(sketch_ref[...])
+    for r in range(points // 128):
+        out_b[128 * r:128 * r + 128, :] = sort_rows(r, sh, sl)
+
+    @pl.loop(1, count)
+    def _(t):
+        to_leaf(t, out_b, in_b, send_b, recv_b).start()
+
+    own_rows = pl.ds(pl.multiple_of(leaf * chunk, chunk), chunk)
+    in_a[0:chunk] = out_a[own_rows, :]
+    in_b[0:chunk] = out_b[own_rows, :]
+
+    def own_side(g, way):
+        peer, slot_at = ((right, 0), (left, 1))[way]
+        rows = pl.ds(g * wide, wide)
+        return pltpu.make_async_remote_copy(
+            src_ref=in_a.at[rows], dst_ref=side.at[slot_at, rows], send_sem=side_send.at[way, g],
+            recv_sem=side_recv.at[slot_at, g], device_id=(leaf, peer), device_id_type=MESH)
+
+    def relay(g, way):
+        peer = (right, left)[way]
+        rows = pl.ds(g * wide + way * (wide // 2), wide // 2)
+        return pltpu.make_async_remote_copy(
+            src_ref=side.at[way, rows], dst_ref=side.at[2, rows], send_sem=side_send.at[2 + way, g],
+            recv_sem=side_recv.at[2 + way, g], device_id=(leaf, peer), device_id_type=MESH)
+
+    scale = -2.0 / feats * math.log2(math.e)
+
+    def arrive(g):
+        @pl.loop(max(1, g * per), (g + 1) * per)
+        def _(t):
+            to_leaf(t, out_a, in_a, send_a, recv_a).wait_recv()
+        own_side(g, 0).start()
+        own_side(g, 1).start()
+        x = in_a[g * wide:g * wide + wide, rank:rank + feats]
+        xh, xl = halves(x)
+        norm = thirds(jnp.sum(x * x, axis=1, keepdims=True) * scale)
+        one = jnp.ones((wide, 1), bf16)
+        sh_, sl_ = halves(x * (-2.0 * scale))
+        row_aug[g * wide:g * wide + wide, :] = jnp.concatenate(
+            [sh_, sh_, sl_, *norm, one, one, one, jnp.zeros((wide, 256 - 3 * feats - 6), bf16)], axis=1)
+
+    def hand_on(g):
+        own_side(g, 0).wait_recv()
+        relay(g, 0).start()
+        own_side(g, 1).wait_recv()
+        relay(g, 1).start()
+
+    def absorb(block):
+        x = block[:, rank:rank + feats]
+        xh, xl = halves(x)
+        norm = thirds(jnp.sum(x * x, axis=1, keepdims=True) * scale)
+        one = jnp.ones((wide, 1), bf16)
+        col_aug = jnp.concatenate(
+            [xh, xl, xh, one, one, one, *norm, jnp.zeros((wide, 256 - 3 * feats - 6), bf16)], axis=1)
+        om = halves(block[:, 0:rank])
+        for a in range(groups):
+            rows = slice(a * wide, a * wide + wide)
+            value = jnp.exp2(mm(row_aug[rows, :], col_aug, NT))
+            acc[rows, :] += dot3(halves(value), om, NN)
+
+    arrive(0)
+    for g in range(1, groups):
+        arrive(g)
+        hand_on(g - 1)
+    acc[...] = jnp.zeros_like(acc)
+
+    @pl.loop(0, groups)
+    def _(g):
+        absorb(in_a[pl.ds(pl.multiple_of(g * wide, wide), wide), :])
+
+    hand_on(groups - 1)
+
+    @pl.loop(0, 2 * groups)
+    def _(i):
+        absorb(side[i // groups, pl.ds(pl.multiple_of((i % groups) * wide, wide), wide), :])
+
+    @pl.loop(0, groups)
+    def _(g):
+        relay(g, 0).wait_recv()
+        relay(g, 1).wait_recv()
+        absorb(side[2, pl.ds(pl.multiple_of(g * wide, wide), wide), :])
+
+    @pl.loop(1, count)
+    def _(t):
+        to_leaf(t, out_b, in_b, send_b, recv_b).wait_recv()
+
+    off = halves(in_b[...] - acc[...])
+    gram_ref[...] = dot3(off, off, TN)
+    back = jnp.where(
+        in_a[:, rank + feats:rank + feats + 1].astype(jnp.int32) == lax.broadcasted_iota(jnp.int32, (points, points), 1),
+        1.0, 0.0).astype(bf16)
+    rhs_ref[...] = mm(off[0], back, TN) + mm(off[1], back, TN)
+
+    @pl.loop(1, count)
+    def _(t):
+        to_leaf(t, out_a, in_a, send_a, recv_a).wait_send()
+        to_leaf(t, out_b, in_b, send_b, recv_b).wait_send()
+
+    @pl.loop(0, groups)
+    def _(g):
+        for way in range(2):
+            own_side(g, way).wait_send()
+            relay(g, way).wait_send()
+
+
+def near_field(slot, features, sketch, omega):
+    feats, points = features.shape
+    rank = sketch.shape[0]
+    count = lax.axis_size("leaf")
+    core = 2
+    z = min(8, count // core)
+    dims = (count // (core * z), z, core)
+    width = rank + 128
+    vm = lambda *shape: pltpu.VMEM(shape, f32)
+    dma = lambda *shape: pltpu.SemaphoreType.DMA(shape)
+    return pl.pallas_call(
+        functools.partial(near_kernel, dims),
+        out_shape=(jax.ShapeDtypeStruct((rank, rank), f32), jax.ShapeDtypeStruct((rank, points), f32)),
+        in_specs=[pl.BlockSpec(memory_space=pltpu.VMEM)] * 4,
+        out_specs=[pl.BlockSpec(memory_space=pltpu.VMEM)] * 2,
+        scratch_shapes=[
+            pltpu.VMEM((points, points), bf16),
+            vm(points, width), vm(points, rank), vm(points, width), vm(points, rank),
+            vm(3, points, width), vm(points, rank), pltpu.VMEM((points, 256), bf16),
+            dma(count), dma(count), dma(count), dma(count), dma(4, 4), dma(4, 4),
+        ],
+        compiler_params=pltpu.CompilerParams(collective_id=0, has_side_effects=True, vmem_limit_bytes=52 << 20),
+    )(slot[None], features, sketch, omega)
 
 
 def per_device(features, sketch, omega, slot, column_order):
-    points = features.shape[1]
-    rank = sketch.shape[0]
-    blk_count = lax.axis_size("blk")
-    leaf_count = lax.axis_size("leaf")
-    sending = jnp.argsort(slot)
-    sorted_slot = slot[sending]
-    position_row = (sorted_slot % points).astype(jnp.float32)[None, :]
-    received = (
-        lax.all_to_all(features[:, sending], "leaf", split_axis=1, concat_axis=1, tiled=True),
-        lax.all_to_all(sketch[:, sending], "leaf", split_axis=1, concat_axis=1, tiled=True),
-        lax.all_to_all(omega[:, sending], "leaf", split_axis=1, concat_axis=1, tiled=True),
-        lax.all_to_all(position_row, "leaf", split_axis=1, concat_axis=1, tiled=True),
-    )
-    arrived_pos = received[3][0].astype(jnp.int32)
-    inverse = jnp.argsort(arrived_pos)
-    tree_feat = received[0][:, inverse]
-    tree_sketch = received[1][:, inverse]
-    tree_omega = received[2][:, inverse]
-    kernel = kernel_block(lax.all_gather(tree_feat, "blk", axis=1, tiled=True), tree_feat)
-    near_field = jnp.dot(
-        lax.all_gather(tree_omega, "blk", axis=1, tiled=True),
-        kernel,
-        precision=lax.Precision.HIGHEST,
-        preferred_element_type=jnp.float32,
-    )
-    off_sketch = tree_sketch - near_field
-    local_gram = lax.dot_general(
-        off_sketch,
-        off_sketch,
-        (((1,), (1,)), ((), ())),
-        precision=lax.Precision.HIGHEST,
-        preferred_element_type=jnp.float32,
-    )
-    gram = lax.psum(local_gram, "blk")
-    leaf_id = lax.axis_index("leaf")
     depth = column_order.shape[0]
-    grams = [gram]
-    running = gram
-    for height in range(depth):
-        grams.append(partner(running, "leaf", height))
-        running = running + grams[-1]
-    second = leaf_id >> jnp.arange(depth, dtype=jnp.int32) & 1
-    leaf_basis, transfers = tri(column_order, jnp.stack(grams), second, off_sketch)
+    gram, turned = near_field(slot, features, sketch, omega)
+    sums = subtree_sums(gram, depth)
+    second = lax.axis_index("leaf") >> jnp.arange(depth, dtype=jnp.int32) & 1
+    leaf_basis, transfers = tri(column_order, sums, second, turned)
     return (leaf_basis, transfers[None])
 
 

time: 349 us -> 157 us (0.45); the launches traced: 342 us -> 155 us
  waiting for transfers between devices: 151 us -> 0 us
  Pallas kernels: 30.9 us -> 153 us
  matrix products: 51.8 us -> 0 us
  starting transfers between devices: 45.6 us -> 0 us
  local copies, waits for them, and re-layouts: 33.8 us -> 1.64 us
  other arithmetic: 14.6 us -> 0.01 us
  between operations: 14.2 us -> 0.68 us
    pallas_call x0 -> x2, Pallas kernels: none -> 122 us  [the longest x1 90.2 us: near_field(): pl.pallas_call(functools.partial(near_kernel, dims), out_shape=(jax.Shape...]
    all_to_all x4 -> x0, waiting for transfers between devices: 52.2 us -> none  [the longest x1 26.2 us: per_device(): lax.all_to_all(sketch[:, sending], 'leaf', split_axis=1, concat_axis=1, t...]
    dot_general x3 -> x0, matrix products: 51.8 us -> none  [the longest x1 34.1 us: per_device(): jnp.dot(lax.all_gather(tree_omega, 'blk', axis=1, tiled=True), kernel, pr...]
    ppermute x6 -> x0, waiting for transfers between devices: 47.5 us -> none  [partner(): return lax.ppermute(block, axis, route)]
    psum x1 -> x0, waiting for transfers between devices: 47.3 us -> none  [per_device(): gram = lax.psum(local_gram, 'blk')]
    all_to_all x4 -> x0, starting transfers between devices: 33.8 us -> none  [the longest x1 12.2 us: per_device(): lax.all_to_all(position_row, 'leaf', split_axis=1, concat_axis=1, tiled=T...]
    gather x10 -> x0, local copies, waits for them, and re-layouts: 30.3 us -> none  [the longest x2 4.77 us: per_device(): tree_sketch = received[1][:, inverse]]
    ppermute x6 -> x0, starting transfers between devices: 11.6 us -> none  [partner(): return lax.ppermute(block, axis, route)]
  transfers between devices with their start and end apart: 13 -> 0, of which waited for: 12 -> 0; matrix products, arithmetic and copies ran while one was open for 15% -> 0% of each run, Pallas kernels for 0% -> 0%
where the time goes in v2:
time: 157 us; the launch traced here: 155 us
  Pallas kernels  153 us (97%)
  local copies, waits for them, and re-layouts  1.64 us (1%)
    pallas_call x1, Pallas kernels, near_field(): pl.pallas_call(functools.partial(near_kernel, dims), out_shape=(jax.Shape...  90.2 us
    pallas_call x1, Pallas kernels, subtree_sums(): pl.pallas_call(sums_kernel, out_shape=jax.ShapeDtypeStruct((depth + 1, ro...  31.4 us
    pallas_call x1, Pallas kernels, tri(): pl.pallas_call(functools.partial(tri_kernel, 2), out_shape=(jax.ShapeDtyp...  31.1 us

profile of v2, /device:TPU:6, one launch (start us, length us, event | category | flops | bytes accessed | tf_op | source)
XLA Modules:
  0.0 155.1 jit_solution(15844688320151884989)
XLA Ops:
  0.6 0.0 copy-start.1
  0.7 0.0 copy-start
  0.7 0.9 copy-done
  1.6 0.0 copy-start.2
  1.6 0.7 copy-done.2
  2.3 90.2 %shard_map.68 = (f32[256,256]{1,0:T(8,128)S(1)}, f32[256,1024]{1,0:T(8,128)S(1)}) custom-call(s32[1,1024]{1,0:T(1,128)S(1)} %bitcast.2, f32[64,1024]{1,0:T(8,128)S(1)} %copy-done, f32[256,1024]{1,0:T(8,128)} %sketch_ref.1, f32[256,1024]{1,0:T(8,128)} %omega_ref.1), custom_call_target="tpu_custom_call" | custom-call | tf_op jit(solution)/shard_map/pallas_call | solution.py:504
  92.5 31.4 %shard_map.69.gram_ref = f32[7,384,128]{2,1,0:T(8,128)S(1)} custom-call(f32[256,256]{1,0:T(8,128)S(1)} %get-tuple-element.6.gram_ref), custom_call_target="tpu_custom_call" | custom-call | tf_op jit(solution)/shard_map/pallas_call | solution.py:301
  124.0 0.0 copy-done.1
  124.0 31.1 %shard_map.70 = (f32[256,1024]{1,0:T(8,128)}, f32[6,512,256]{2,1,0:T(8,128)}) custom-call(s32[6,256]{1,0:T(8,128)S(1)} %copy-done.1, f32[7,384,128]{2,1,0:T(8,128)S(1)} %shard_map.69.gram_ref, s32[6]{0:T(128)S(1)} %shift-right-arithmetic_and_fusion.second_ref, f32[256,1024]{1,0:T(8,128)S(1)} %get-tuple-element.7.rhs_ref), custom_call_target="tpu_custom_call" | custom-call | tf_op jit(solution)/shard_map/pallas_call | solution.py:197
  (1 shorter events, 0.0 us)
Async XLA Ops:
  0.6 123.3 %copy-start.1 = (s32[6,256]{1,0:T(8,128)S(1)}, s32[6,256]{1,0:T(8,128)}, u32[]{:S(2)}) copy-start(s32[6,256]{1,0:T(8,128)} %order_ref.1) | copy-start | bytes 18436
  0.7 1.0 copy-start
  1.6 0.7 copy-start.2
